TPU v7x, 32 devices: a whole 2x2x4 slice. The times are simulated.
32 devices in a mesh: groups: 2 (over y), mem: 8 (over z, x), lat: 2 (over core).
Axes of the slice: x: 2, y: 2, z: 4, core: 2. Of those that a mesh axis runs over, the one named last changes fastest.
Arguments:
- state: bfloat16 [64, 8, 64, 512], P(('groups', 'mem'), None, 'lat'), parts along dimension 0, may hold values from -6 to 6
- counts: int32 [16], P(('groups', 'mem')), parts along dimension 0, may hold values from 1 to 4, 16 in all
- east_wind: float32 [128, 512], P(('groups', 'lat')), parts along dimension 0, may hold values from -0.48 to 0.48
- north_wind: float32 [128, 512], P(('groups', 'lat')), parts along dimension 0, may hold values from -0.48 to 0.48
- obs_cells: int32 [4, 32768], P(('groups', 'lat')), parts along dimension 0, may hold values from 0 to 16383
- obs_mask: int32 [4, 32768], P(('groups', 'lat')), parts along dimension 0, may hold values 0 or 1
- obs_values: float32 [4, 32768], P(('groups', 'lat')), parts along dimension 0, may hold values from -6 to 6
- obs_error: float32 [4, 32768], P(('groups', 'lat')), parts along dimension 0, may hold values from 0.2 to 2
- relax: float32 [8], replicated, may hold values from 0.3 to 0.9
Outputs:
- new_state: bfloat16 [64, 8, 64, 512], P(('groups', 'mem'), None, 'lat'), parts along dimension 0
- analysis_mean: bfloat16 [16, 64, 512], P('groups', 'lat'), parts along dimension 0
There are 2 independent parts, one for each index of `groups`. A program takes and returns all parts, laid end to end along the dimension named above; an argument that names none is the same for every part. Nothing has to cross between parts.
Inputs may be any that keep to these rules, and one draw needn't show every extreme that they name: counts over the mem axis add up to 16, and some mem index holds 4 members.
All inputs are finite; a program needn't handle non-finite values. No bound on the sum of `counts` or of `obs_mask` on one device may be relied on, other than what follows from the above.
Results may differ from a plain program's by a relative error of at most 0.001.
The roundings to bfloat16 on the way count: a program that leaves them out, or rounds other values in their place, can miss the bound.
Values may be sent and summed in bfloat16 or wider, within the bound.
No kernel may reach another device: no remote copies, remote signals or barrier semaphores. Data moves between devices by JAX's collectives and lax.ppermute only.
A program may use at most 128 MiB of HBM per device.

v0:
```python
import functools

import jax
import jax.numpy as jnp
import ml_dtypes
import numpy as np
from jax import lax
from jax.experimental import pallas as pl
from jax.experimental.pallas import tpu as pltpu
from jax.sharding import PartitionSpec as P

STEPS = 4
SMOOTH = 16
LOG_TWO_PI = 1.8378770664093453
LANES = 128
TILE = 8
PARTS = 5
CHUNK_ROWS = 32
PACK = 16
BEGIN_STEPS = 2
LATER_FIELDS = 1
PAIR = 2
LINE = 4
SHARE_ORDER = (0, 6, 7, 2, 1, 4, 5, 3)


VMEM = pl.BlockSpec(memory_space=pltpu.VMEM)
PARAMS = pltpu.CompilerParams(vmem_limit_bytes=24 * 1024 * 1024)
EDGE_VMEM = 63 * 1024 * 1024


def kernel_matrix(offset):
    values = np.exp(-((2.0 * offset.astype(np.float32) / SMOOTH) ** 2))
    return np.where(np.abs(offset) <= SMOOTH, values, 0.0).astype(np.float32)


def split_constant(matrix):
    parts = []
    for _ in range(3):
        parts.append(matrix.astype(ml_dtypes.bfloat16))
        matrix = matrix - parts[-1].astype(np.float32)
    return jnp.asarray(np.stack(parts))


def split_two(x):
    high = x.astype(jnp.bfloat16).astype(jnp.float32)
    return high, x - high


def spread_terms(cells_ref, mask_ref, values_ref, error_ref, rows_ref, rows, width):
    half = width // 2
    cells = cells_ref[...]
    used = mask_ref[...].astype(jnp.float32)
    values = values_ref[...]
    error = error_ref[...]
    inverse = used / (error * error)
    first = inverse * values
    second = first * values + used * (2.0 * jnp.log(error) + LOG_TWO_PI)
    row = cells // width
    column = cells % width
    high = (column // half * rows + row).astype(jnp.float32)
    low = (column % half).astype(jnp.float32)
    for k, x in enumerate(split_two(inverse) + split_two(first) + (second, high, low)):
        rows_ref[k] = x


def add_observations(step, size, rows_ref, acc_ref):
    highs, lows = acc_ref.shape[0] // PARTS, acc_ref.shape[1]

    def steps_of(count):
        base = lax.broadcasted_iota(jnp.int32, (PACK, LANES), 0)
        return [
            (base + PACK * i).astype(jnp.float32).astype(jnp.bfloat16) for i in range(count // PACK)
        ]

    high_iota, low_iota = steps_of(highs), steps_of(lows)
    zero = jnp.zeros((PACK, LANES), jnp.bfloat16)
    one = jnp.ones((PACK, LANES), jnp.bfloat16)
    here = pl.ds(pl.multiple_of(step * size, size), size)
    held = [rows_ref[k, here, :] for k in range(PARTS + 2)]
    left, right = [], []
    for r in range(size):
        spread = [
            jnp.broadcast_to(x[r : r + 1, :], (PACK, LANES)).astype(jnp.bfloat16) for x in held
        ]
        high_row, low_row = spread[PARTS:]
        hit = [iota == high_row for iota in high_iota]
        left.append(
            jnp.concatenate([jnp.where(h, part, zero) for part in spread[:PARTS] for h in hit], axis=0)
        )
        right.append(
            jnp.concatenate([jnp.where(iota == low_row, one, zero) for iota in low_iota], axis=0)
        )
    acc_ref[...] += lax.dot_general(
        jnp.concatenate(left, axis=1),
        jnp.concatenate(right, axis=1),
        (((1,), (1,)), ((), ())),
        preferred_element_type=jnp.float32,
    )


def grids_of(acc_ref, rows):
    highs = 2 * rows

    def part_sum(indices):
        total = acc_ref[pl.ds(indices[-1] * highs, highs), :]
        for i in indices[-2::-1]:
            total = total + acc_ref[pl.ds(i * highs, highs), :]
        return jnp.concatenate([total[0:rows], total[rows:highs]], axis=1)

    return [part_sum(indices) for indices in ((0, 1), (2, 3), (4,))]


def begin_kernel(rows, width, steps, cells_ref, mask_ref, values_ref, error_ref, rows_ref, acc_ref):
    spread_terms(cells_ref, mask_ref, values_ref, error_ref, rows_ref, rows, width)
    acc_ref[...] = jnp.zeros_like(acc_ref)

    def body(step, carry):
        add_observations(step, CHUNK_ROWS, rows_ref, acc_ref)
        return carry

    lax.fori_loop(0, steps, body, 0)


def wind_parts(east_ref, north_ref, wind_halo_ref):
    east = jnp.concatenate([east_ref[...], wind_halo_ref[0]], axis=0)
    north = jnp.concatenate([north_ref[...], wind_halo_ref[1]], axis=0)
    west, south = jnp.maximum(east, 0.0), jnp.maximum(north, 0.0)
    east, north = -jnp.minimum(east, 0.0), -jnp.minimum(north, 0.0)
    return 1.0 - west - east - south - north, west, east, south, north


def edge_kernel(state_in, east_in, north_in, out_ref, state_ref, wind_ref, sems):
    slots, fields, rows, width = state_in.shape
    place = lax.axis_index("lat")
    lower = place == 0
    here = pl.ds(pl.multiple_of((1 - place) * (rows - 2 * TILE), 2 * TILE), 2 * TILE)
    copies = [
        pltpu.make_async_copy(state_in.at[:, :, here], state_ref, sems.at[0]),
        pltpu.make_async_copy(east_in.at[here], wind_ref.at[0], sems.at[1]),
        pltpu.make_async_copy(north_in.at[here], wind_ref.at[1], sems.at[2]),
    ]
    for copy in copies:
        copy.start()
    low_row = lax.broadcasted_iota(jnp.int32, (TILE, width), 0) < TILE // 2
    keep = low_row != lower

    def edge(block):
        return jnp.where(keep, jnp.where(lower, block[TILE:], block[0:TILE]), 0.0)

    for copy in copies:
        copy.wait()
    for s in range(slots):
        for f in range(fields):
            out_ref[s * fields + f] = edge(state_ref[s, f].astype(jnp.float32))
    for i in range(2):
        out_ref[slots * fields + i] = edge(wind_ref[i])


def store_winds(east_ref, north_ref, halo_ref, count, winds_ref):
    for i, part in enumerate(wind_parts(east_ref, north_ref, halo_ref.at[pl.ds(count, 2)])):
        winds_ref[i] = part


def advect_field(state_ref, halo_ref, winds_ref, buffer_ref, f, adv_ref, place, as_written=False):
    slots, fields, rows, width = state_ref.shape
    across, band_tiles = width // LANES, rows // TILE
    tiles = band_tiles + 1
    lane = lax.broadcasted_iota(jnp.int32, (TILE, LANES), 1)
    first, last = lane == 0, lane == LANES - 1

    def columns(l):
        return slice(l * LANES, (l + 1) * LANES)

    def put(side, k, l, v, value):
        copies = [v + 1] + ([0] if v == tiles - 1 else []) + ([tiles + 1] if v == 0 else [])
        for at in copies:
            buffer_ref[side, k, l, at * TILE : (at + 1) * TILE, :] = value

    for k in range(slots):
        x = state_ref[k, f].astype(jnp.float32)
        halo = halo_ref[k * fields + f]
        for l in range(across):
            for v in range(band_tiles):
                put(0, k, l, v, x[v * TILE : (v + 1) * TILE, columns(l)])
            put(0, k, l, band_tiles, halo[:, columns(l)])

    done = [[] for _ in range(slots)]
    for step in range(STEPS):
        side = step % 2
        ends = step == STEPS - 1
        for v in range(band_tiles if ends else tiles):
            cells = []
            for k in range(slots):

                def row_tile(offset):
                    start = (v + 1) * TILE + offset
                    return [buffer_ref[side, k, l, start : start + TILE, :] for l in range(across)]

                x = row_tile(0)
                west = [pltpu.roll(value, 1, 1) for value in x]
                east = [pltpu.roll(value, LANES - 1, 1) for value in x]
                cells.append(
                    (
                        x,
                        [jnp.where(first, west[l - 1], west[l]) for l in range(across)],
                        [jnp.where(last, east[(l + 1) % across], east[l]) for l in range(across)],
                        row_tile(-1),
                        row_tile(1),
                    )
                )
            stepped = [[] for _ in range(slots)]
            for l in range(across):
                here = slice(v * TILE, (v + 1) * TILE)
                centre, *winds = [winds_ref[c, here, columns(l)] for c in range(5)]
                for k in range(slots):
                    x, west, east, south, north = [values[l] for values in cells[k]]
                    if as_written:
                        x = (
                            x
                            - winds[0] * (x - west)
                            + winds[1] * (east - x)
                            - winds[2] * (x - south)
                            + winds[3] * (north - x)
                        )
                    else:
                        x = (
                            centre * x
                            + winds[0] * west
                            + winds[1] * east
                            + winds[2] * south
                            + winds[3] * north
                        )
                    if ends:
                        stepped[k].append(x)
                    else:
                        put(1 - side, k, l, v, x)
            if ends:
                for k in range(slots):
                    done[k].append(jnp.concatenate(stepped[k], axis=1))
    for k in range(slots):
        for v in range(0, band_tiles, 2):
            block = jnp.concatenate(done[k][v : v + 2], axis=0)
            adv_ref[k, place, v * TILE : (v + 2) * TILE, :] = block.astype(jnp.bfloat16)


def parts_of(x):
    high = x.astype(jnp.bfloat16)
    rest = x - high.astype(jnp.float32)
    middle = rest.astype(jnp.bfloat16)
    return [high, middle, (rest - middle.astype(jnp.float32)).astype(jnp.bfloat16)]


def product(left, right):
    rows = left[0].shape[0]
    total = None
    for p in reversed(range(3)):
        pieces = jnp.dot(
            jnp.concatenate(left[: 3 - p], axis=0), right[p], preferred_element_type=jnp.float32
        )
        for q in reversed(range(3 - p)):
            term = pieces[q * rows : (q + 1) * rows]
            total = term if total is None else total + term
    return total


def first_kernel(
    steps, state_ref, halo_ref, east_ref, north_ref, terms_ref, acc_in_ref, lat_ref, lon_ref,
    adv_ref, own_ref, send_ref, acc_ref, winds_ref, buffer_ref,
):
    slots, fields, rows, width = state_ref.shape
    store_winds(east_ref, north_ref, halo_ref, slots * fields, winds_ref)
    acc_ref[...] = acc_in_ref[...]
    held = adv_ref.shape[1]
    total = terms_ref.shape[1] // CHUNK_ROWS

    def advect_next(f, as_written):
        advect_field(state_ref, halo_ref, winds_ref, buffer_ref, f, adv_ref, f, as_written)

    def both(as_written):
        def body(i, carry):
            add_observations(steps + i, CHUNK_ROWS, terms_ref, acc_ref)
            advect_next(i, as_written)
            return carry

        return body

    def observe(step, carry):
        add_observations(step, CHUNK_ROWS, terms_ref, acc_ref)
        return carry

    shared = min(held, total - steps)
    if shared:
        lax.fori_loop(0, 1, both(True), 0)
        lax.fori_loop(1, shared, both(False), 0)
    if steps + shared < total:
        lax.fori_loop(steps + shared, total, observe, 0)
    for f in range(shared, held):
        advect_next(f, f == 0)

    inverse, first, second = grids_of(acc_ref, rows)
    logliks = []
    for s in range(slots):
        value = adv_ref[s, 0].astype(jnp.float32)
        logliks.append(-0.5 * (inverse * value * value - 2.0 * first * value + second))
    count = slots * rows
    edge = count + jnp.where(lax.axis_index("lat") == 0, 0, slots * SMOOTH)
    edge = pl.ds(pl.multiple_of(edge, SMOOTH), slots * SMOOTH)
    lat_parts = [
        jnp.concatenate([lat_ref[p, 0:count], lat_ref[p, edge]], axis=0) for p in range(3)
    ]
    along = product(parts_of(jnp.concatenate(logliks, axis=0)), [lon_ref[p] for p in range(3)])
    scores = product(lat_parts, parts_of(along))
    for s in range(slots):
        own_ref[s] = scores[s * rows : (s + 1) * rows]
        send_ref[s] = scores[count + s * SMOOTH : count + (s + 1) * SMOOTH]


def rest_kernel(
    state_ref, halo_ref, east_ref, north_ref, adv_ref, winds_ref, buffer_ref
):
    slots, fields = state_ref.shape[:2]
    held = adv_ref.shape[1]
    store_winds(east_ref, north_ref, halo_ref, slots * fields, winds_ref)


    def body(i, carry):
        f = fields - held + i
        advect_field(state_ref, halo_ref, winds_ref, buffer_ref, f, adv_ref, i)
        return carry

    lax.fori_loop(0, held, body, 0)


def field_ref(adv_first_ref, adv_rest_ref, s, f):
    held = adv_first_ref.shape[1]
    return adv_first_ref.at[s, f] if f < held else adv_rest_ref.at[s, f - held]


def weigh_all_kernel(
    counts_ref, own_ref, recv_ref, adv_first_ref, adv_rest_ref, parts_ref
):
    slots, rows, width = own_ref.shape
    fields = adv_first_ref.shape[1] + adv_rest_ref.shape[1]
    across = width // LANES
    members, _, held, _ = parts_ref.shape

    def store(row_tile, index, value):
        for l in range(across):
            tile = value[:, l * LANES : (l + 1) * LANES]
            row = (row_tile * across + l) * TILE
            for k in range(0, TILE, min(held, TILE)):
                chunk, at = divmod(row + k, held)
                parts_ref[chunk, index, at : at + min(held, TILE)] = tile[k : k + min(held, TILE)]

    lower = lax.axis_index("lat") == 0
    for t in range(rows // TILE):
        here = slice(t * TILE, (t + 1) * TILE)
        near = (t * TILE) % SMOOTH
        scores = []
        for s in range(slots):
            recv = recv_ref[s, near : near + TILE, :]
            at_this_edge = lower if t * TILE >= rows - SMOOTH else jnp.logical_not(lower)
            score = own_ref[s, here, :] + jnp.where(at_this_edge, recv, 0.0)
            scores.append(jnp.where(s < counts_ref[0:1, 0:1], score, -jnp.inf))
        peak = functools.reduce(jnp.maximum, scores)
        gains = [jnp.exp(score - peak) for score in scores]
        total = functools.reduce(jnp.add, gains)
        store(t, 0, peak + jnp.log(total))
        gains = [gain / total for gain in gains]
        for f in range(fields):
            mean = None
            for s in range(slots):
                ref = field_ref(adv_first_ref, adv_rest_ref, s, f)
                pair = slice(t // 2 * 2 * TILE, (t // 2 + 1) * 2 * TILE)
                value = ref[pair, :].astype(jnp.float32)[t % 2 * TILE : (t % 2 + 1) * TILE]
                term = gains[s] * value
                mean = term if mean is None else mean + term
            store(t, 1 + f, mean)


def weigh_kernel(
    counts_ref, own_ref, recv_ref, adv_first_ref, adv_rest_ref, *out_refs
):
    slots, rows, width = own_ref.shape
    fields = adv_first_ref.shape[1] + adv_rest_ref.shape[1]
    half = width // PAIR
    lower = lax.axis_index("lat") == 0
    member = lax.axis_index("mem")
    even_side = member % PAIR == 0
    for distance in range(LINE):
        tile = (member // PAIR) ^ distance
        here = pl.ds(pl.multiple_of(tile * TILE, TILE), TILE)
        near = pl.ds(pl.multiple_of(tile % 2 * TILE, TILE), TILE)
        pair = pl.ds(pl.multiple_of(tile // 2 * (2 * TILE), 2 * TILE), 2 * TILE)
        even_tile = tile % 2 == 0
        at_edge = lower == (tile * TILE >= rows - SMOOTH)
        keep_ref, send_ref = out_refs[distance], out_refs[LINE + distance]

        def store(index, value):
            left, right = value[:, 0:half], value[:, half:width]
            keep_ref[index] = jnp.where(even_side, left, right)
            send_ref[index] = jnp.where(even_side, right, left)

        scores = []
        for s in range(slots):
            score = own_ref[s, here, :] + jnp.where(at_edge, recv_ref[s, near, :], 0.0)
            scores.append(jnp.where(s < counts_ref[0:1, 0:1], score, -jnp.inf))
        peak = functools.reduce(jnp.maximum, scores)
        gains = [jnp.exp(score - peak) for score in scores]
        total = functools.reduce(jnp.add, gains)
        store(0, peak + jnp.log(total))
        gains = [gain / total for gain in gains]
        for f in range(fields):
            mean = None
            for s in range(slots):
                ref = field_ref(adv_first_ref, adv_rest_ref, s, f)
                value = ref[pair, :].astype(jnp.float32)
                term = gains[s] * jnp.where(even_tile, value[0:TILE], value[TILE:])
                mean = term if mean is None else mean + term
            store(1 + f, mean)


def merge_values(refs):
    peak = functools.reduce(jnp.maximum, [ref[0] for ref in refs])
    weights = [jnp.exp(ref[0] - peak) for ref in refs]
    total = functools.reduce(jnp.add, weights)
    shares = [weight / total for weight in weights]
    means = [
        functools.reduce(jnp.add, [share * ref[q] for share, ref in zip(shares, refs)])
        for q in range(1, refs[0].shape[0])
    ]
    return peak + jnp.log(total), means


def merge_kernel(*refs):
    out_ref = refs[-1]
    log_weight, means = merge_values(refs[:-1])
    out_ref[0] = log_weight
    for f, mean in enumerate(means):
        out_ref[1 + f] = mean


def finish_kernel(*refs):
    merged_ref = refs[-1]
    parts = refs[:-1]
    if len(parts) == 1:
        parts = [parts[0].at[d] for d in range(parts[0].shape[0])]
    for f, mean in enumerate(merge_values(parts)[1]):
        merged_ref[f] = mean


def relaxed(value, merged, factor, live):
    value = value.astype(jnp.float32)
    return jnp.where(live, value + factor * (merged - value), 0.0).astype(jnp.bfloat16)


def relax_all_kernel(
    counts_ref, relax_ref, adv_first_ref, adv_rest_ref, whole_ref, new_ref, mean_ref
):
    _, fields, rows, width = new_ref.shape
    across = width // LANES
    held = whole_ref.shape[2]

    def tile(f, row):
        if held >= TILE:
            return whole_ref[row // held, f, row % held : row % held + TILE]
        return jnp.concatenate([whole_ref[(row + k) // held, f] for k in range(0, TILE, held)], axis=0)

    for f in range(fields):
        merged = jnp.concatenate(
            [
                jnp.concatenate([tile(f, (t * across + l) * TILE) for l in range(across)], axis=1)
                for t in range(rows // TILE)
            ],
            axis=0,
        )
        mean_ref[f] = merged.astype(jnp.bfloat16)
        for s in range(new_ref.shape[0]):
            value = field_ref(adv_first_ref, adv_rest_ref, s, f)[...]
            new_ref[s, f] = relaxed(value, merged, relax_ref[f], s < counts_ref[0:1, 0:1])


def relax_kernel(counts_ref, relax_ref, adv_first_ref, adv_rest_ref, *refs):
    share_refs, (new_out, mean_out, merged_ref, new_ref, mean_ref, sems) = refs[:-6], refs[-6:]
    slots, fields, rows, width = new_ref.shape
    share_of = dict(zip(SHARE_ORDER, share_refs))
    member = lax.axis_index("mem")
    even_side = member % PAIR == 0
    copies = []
    for f in range(fields):
        for distance in range(LINE):
            tile = (member // PAIR) ^ distance
            same = share_of[PAIR * distance][f]
            other = share_of[PAIR * distance + 1][f]
            left = jnp.where(even_side, same, other)
            right = jnp.where(even_side, other, same)
            merged_ref[f, pl.ds(pl.multiple_of(tile * TILE, TILE), TILE), :] = jnp.concatenate(
                [left, right], axis=1
            )
        merged = merged_ref[f]
        mean_ref[f] = merged.astype(jnp.bfloat16)
        for s in range(slots):
            value = field_ref(adv_first_ref, adv_rest_ref, s, f)[...]
            new_ref[s, f] = relaxed(value, merged, relax_ref[f], s < counts_ref[0:1, 0:1])
        copies.append(pltpu.make_async_copy(new_ref.at[:, f], new_out.at[:, f], sems.at[0, f]))
        copies.append(pltpu.make_async_copy(mean_ref.at[f], mean_out.at[f], sems.at[1, f]))
        for copy in copies[-2:]:
            copy.start()
    for copy in copies:
        copy.wait()


def call(kernel, ins, outs, scratch=(), **cost):
    return pl.pallas_call(
        kernel,
        out_shape=[jax.ShapeDtypeStruct(shape, dtype) for shape, dtype in outs],
        in_specs=ins,
        out_specs=[VMEM] * len(outs),
        scratch_shapes=list(scratch),
        compiler_params=PARAMS,
        cost_estimate=pl.CostEstimate(**cost),
    )


def on_device(
    state, counts, east_wind, north_wind, obs_cells, obs_mask, obs_values, obs_error, relax
):
    slots, fields, rows, width = state.shape
    f32, bf16 = jnp.float32, jnp.bfloat16
    swap = [(0, 1), (1, 0)]
    (message,) = pl.pallas_call(
        edge_kernel,
        out_shape=[jax.ShapeDtypeStruct((slots * fields + 2, TILE, width), f32)],
        in_specs=[pl.BlockSpec(memory_space=pltpu.HBM)] * 3,
        out_specs=[VMEM],
        scratch_shapes=[
            pltpu.VMEM((slots, fields, 2 * TILE, width), bf16),
            pltpu.VMEM((2, 2 * TILE, width), f32),
            pltpu.SemaphoreType.DMA((3,)),
        ],
        compiler_params=pltpu.CompilerParams(vmem_limit_bytes=EDGE_VMEM),
        cost_estimate=pl.CostEstimate(
            flops=0, bytes_accessed=6 * slots * fields * TILE * width, transcendentals=0
        ),
    )(state, east_wind, north_wind)
    halo = lax.ppermute(message, "lat", swap)

    observations = obs_cells.shape[1]
    flat = [
        x.reshape(observations // LANES, LANES) for x in (obs_cells, obs_mask, obs_values, obs_error)
    ]
    acc_shape = (PARTS * 2 * rows, width // 2)
    all_steps = observations // (LANES * CHUNK_ROWS)
    begin_steps = min(BEGIN_STEPS, all_steps)
    observe_flops = 2 * PARTS * rows * width * LANES * CHUNK_ROWS
    terms, begun = call(
        functools.partial(begin_kernel, rows, width, begin_steps),
        [VMEM] * 4,
        [((PARTS + 2, observations // LANES, LANES), f32), (acc_shape, f32)],
        flops=observe_flops * begin_steps,
        bytes_accessed=16 * observations,
        transcendentals=observations,
    )(*flat)

    index = np.arange(rows)
    own = index[None, :] - index[:, None]
    upper_side = index[None, :] - (index[:SMOOTH, None] + rows)
    lower_side = index[None, :] - (index[rows - SMOOTH :, None] - rows)
    same_slot = np.eye(slots, dtype=np.float32)
    lat_kernel = split_constant(
        np.concatenate(
            [np.kron(same_slot, kernel_matrix(x)) for x in (own, upper_side, lower_side)]
        )
    )
    distance = np.abs(np.arange(width)[:, None] - np.arange(width)[None, :])
    lon_kernel = split_constant(kernel_matrix(np.minimum(distance, width - distance)))

    advect_scratch = [
        pltpu.VMEM((5, rows + TILE, width), f32),
        pltpu.VMEM((2, slots, width // LANES, rows + 3 * TILE, LANES), f32),
    ]
    advect_flops = STEPS * 16 * slots * rows * width
    adv_first, own_scores, edge_scores = call(
        functools.partial(first_kernel, begin_steps),
        [VMEM] * 8,
        [
            ((slots, fields - LATER_FIELDS, rows, width), bf16),
            ((slots, rows, width), f32),
            ((slots, SMOOTH, width), f32),
        ],
        [pltpu.VMEM(acc_shape, f32)] + advect_scratch,
        flops=observe_flops * (all_steps - begin_steps) + advect_flops * (fields - LATER_FIELDS),
        bytes_accessed=4 * width * width,
        transcendentals=0,
    )(state, halo, east_wind, north_wind, terms, begun, lat_kernel, lon_kernel)
    received = lax.ppermute(edge_scores, "lat", swap)

    (adv_rest,) = call(
        rest_kernel,
        [VMEM] * 4,
        [((slots, LATER_FIELDS, rows, width), bf16)],
        advect_scratch,
        flops=advect_flops * LATER_FIELDS,
        bytes_accessed=4 * slots * fields * rows * width,
        transcendentals=0,
    )(state, halo, east_wind, north_wind)

    members = lax.axis_size("mem")
    counts = jnp.broadcast_to(jnp.clip(counts, 1, slots)[0], (TILE, LANES))
    factors = jnp.broadcast_to(relax[:, None, None], (fields, 1, width))
    quantities = fields + 1
    direct = (members, rows, width % (PAIR * LANES)) == (PAIR * LINE, LINE * TILE, 0)
    chunk = (TILE, width // PAIR) if direct else (rows * width // LANES // members, LANES)
    cells = chunk[0] * chunk[1]

    def weigh(kernel, outs):
        return call(
            kernel,
            [VMEM] * 5,
            outs,
            flops=4 * slots * fields * rows * width,
            bytes_accessed=4 * slots * fields * rows * width,
            transcendentals=slots * rows * width,
        )(counts, own_scores, received, adv_first, adv_rest)

    def merge(kernel, pieces, out):
        size = quantities * cells * (len(pieces) if direct else members)
        return call(
            kernel,
            [VMEM] * len(pieces),
            [out],
            flops=4 * size,
            bytes_accessed=4 * size,
            transcendentals=size // quantities,
        )(*pieces)[0]

    def swapped(x, offset):
        return lax.ppermute(x, "mem", [(m, m ^ offset) for m in range(members)])

    merged_chunk = ((fields,) + chunk, f32)
    new_shape, mean_shape = (slots, fields, rows, width), (fields, rows, width)
    outs = [(new_shape, bf16), (mean_shape, bf16)]
    if direct:
        piece = ((quantities,) + chunk, f32)
        parts = weigh(weigh_kernel, [piece] * (PAIR * LINE))
        paired = [None] * LINE
        for j in reversed(range(LINE)):
            paired[j] = merge(merge_kernel, [parts[j], swapped(parts[LINE + j], 1)], piece)
        pieces = [paired[0]] + [swapped(paired[j], PAIR * j) for j in range(1, LINE)]
        merged = merge(finish_kernel, pieces, merged_chunk)
        far = LINE - 1
        sent = {0: merged}
        for offset in SHARE_ORDER[1:]:
            through = offset ^ 1 if offset % PAIR and offset // PAIR < far else 0
            sent[offset] = swapped(sent[through], offset ^ through)
        size = slots * fields * rows * width
        new_state, mean = pl.pallas_call(
            relax_kernel,
            out_shape=[jax.ShapeDtypeStruct(*out) for out in outs],
            in_specs=[VMEM] * (4 + len(sent)),
            out_specs=[pl.BlockSpec(memory_space=pl.ANY)] * 2,
            scratch_shapes=[
                pltpu.VMEM((fields, rows, width), f32),
                pltpu.VMEM(new_shape, bf16),
                pltpu.VMEM(mean_shape, bf16),
                pltpu.SemaphoreType.DMA((2, fields)),
            ],
            compiler_params=PARAMS,
            cost_estimate=pl.CostEstimate(flops=4 * size, bytes_accessed=4 * size, transcendentals=0),
        )(counts, factors, adv_first, adv_rest, *[sent[i] for i in SHARE_ORDER])
    else:
        (parts,) = weigh(weigh_all_kernel, [((members, quantities) + chunk, f32)])
        got = lax.all_to_all(parts, "mem", 0, 0, tiled=True)
        whole = lax.all_gather(merge(finish_kernel, [got], merged_chunk), "mem")
        new_state, mean = call(
            relax_all_kernel,
            [VMEM] * 5,
            outs,
            flops=4 * slots * fields * rows * width,
            bytes_accessed=4 * slots * fields * rows * width,
            transcendentals=0,
        )(counts, factors, adv_first, adv_rest, whole)
    return (new_state, mean)


def solution(mesh):
    return jax.shard_map(
        on_device,
        mesh=mesh,
        in_specs=(
            P(("groups", "mem"), None, "lat", None),
            P(("groups", "mem")),
            P(("groups", "lat"), None),
            P(("groups", "lat"), None),
            P(("groups", "lat"), None),
            P(("groups", "lat"), None),
            P(("groups", "lat"), None),
            P(("groups", "lat"), None),
            P(),
        ),
        out_specs=(P(("groups", "mem"), None, "lat", None), P("groups", "lat", None)),
        check_vma=False,
    )
```

profile of v0, /device:TPU:0, one launch (start us, length us, event | category | flops | bytes accessed | tf_op | source)
XLA Modules:
  0.0 47.4 jit_solution(12774251774280809742)
XLA Ops:
  0.7 2.0 %shard_map.122 = f32[34,8,512]{2,1,0:T(8,128)} custom-call(bf16[4,8,32,512]{3,2,1,0:T(8,128)(2,1)} %state_ref.3, f32[32,512]{1,0:T(8,128)} %east_ref.3, f32[32,512]{1,0:T(8,128)} %north_ref.3), custom_call_target="tpu_custom_call" | custom-call | bytes 786432 | tf_op jit(solution)/shard_map/pallas_call | solution.py:532
  2.7 0.5 %collective-permute-start = (f32[34,8,512]{2,1,0:T(8,128)}, f32[34,8,512]{2,1,0:T(8,128)S(1)}, u32[]{:S(2)}, u32[]{:S(2)}) collective-permute-start(f32[34,8,512]{2,1,0:T(8,128)} %shard_map.122), channel_id=1, source_target_pairs={{0,1},{1,0},{2,3},{3,2},{4,5},{5,4},{6,7},{7,6},{8,9},{9,8},{10,11... | collective-permute-start | bytes 1671176 | tf_op jit(solution)/shard_map/ppermute | solution.py:547
  3.3 2.1 %shard_map.123 = (f32[7,256,128]{2,1,0:T(8,128)S(1)}, f32[320,256]{1,0:T(8,128)S(1)}) custom-call(s32[256,128]{1,0:T(8,128)S(1)} %bitcast.5, s32[256,128]{1,0:T(8,128)S(1)} %bitcast.6, f32[256,128]{1,0:T(8,128)S(1)} %bitcast.7, f32[256,128]{1,0:T(8,128)S(1)} %bitcast.8), custom_call_target="tpu_custom_call" | custom-call | flops 1342177280 | bytes 524288 | tf_op jit(solution)/shard_map/pallas_call | solution.py:557
  5.4 8.1 %shard_map.124 = (bf16[4,7,32,512]{3,2,1,0:T(8,128)(2,1)S(1)}, f32[4,32,512]{2,1,0:T(8,128)S(1)}, f32[4,16,512]{2,1,0:T(8,128)S(1)}) custom-call(bf16[4,8,32,512]{3,2,1,0:T(8,128)(2,1)S(1)} %copy-done, f32[34,8,512]{2,1,0:T(8,128)S(1)} %collective-permute-done.halo_ref, f32[32,512]{1,0:T(8,128)S(1)} %copy-done.1, f32[32,512]{1,0:T(8,128)S(1)} %copy-done.2, ...), custom_call_target="tpu_custom_call" | custom-call | flops 4055891968 | bytes 1048576 | tf_op jit(solution)/shard_map/pallas_call | solution.py:584
  14.3 0.7 %shard_map.125.adv_rest_ref = bf16[4,1,32,512]{3,2,1,0:T(8,128)(2,1)S(1)} custom-call(bf16[4,8,32,512]{3,2,1,0:T(8,128)(2,1)S(1)} %copy-done, f32[34,8,512]{2,1,0:T(8,128)S(1)} %collective-permute-done.halo_ref, f32[32,512]{1,0:T(8,128)S(1)} %copy-done.1, f32[32,512]{1,0:T(8,128)S(1)} %copy-done.2), custom_call_target="tpu_custom_call" | custom-call | flops 4194304 | bytes 2097152 | tf_op jit(solution)/shard_map/pallas_call | solution.py:599
  15.5 3.0 %collective-permute-start.7 = (f32[9,8,256]{2,1,0:T(8,128)S(1)}, f32[9,8,256]{2,1,0:T(8,128)S(1)}, u32[]{:S(2)}, u32[]{:S(2)}) collective-permute-start(f32[9,8,256]{2,1,0:T(8,128)S(1)} %get-tuple-element.27), channel_id=1, source_target_pairs={{0,2},{2,0},{4,6},{6,4},{8,10},{10,8},{12,14},{14,12},{1,3},{3,1},... | collective-permute-start | bytes 221192 | tf_op jit(solution)/shard_map/ppermute | solution.py:639
  18.6 1.9 %collective-permute-start.3 = (f32[9,8,256]{2,1,0:T(8,128)S(1)}, f32[9,8,256]{2,1,0:T(8,128)S(1)}, u32[]{:S(2)}, u32[]{:S(2)}) collective-permute-start(f32[9,8,256]{2,1,0:T(8,128)S(1)} %get-tuple-element.23), channel_id=1, source_target_pairs={{0,2},{2,0},{4,6},{6,4},{8,10},{10,8},{12,14},{14,12},{1,3},{3,1},... | collective-permute-start | bytes 221192 | tf_op jit(solution)/shard_map/ppermute | solution.py:639
  20.6 0.5 %collective-permute-done.7.refs_1_ = f32[9,8,256]{2,1,0:T(8,128)S(1)} collective-permute-done((f32[9,8,256]{2,1,0:T(8,128)S(1)}, f32[9,8,256]{2,1,0:T(8,128)S(1)}, u32[]{:S(2)}, u32[]{:S(2)}) %collective-permute-start.7) | collective-permute-done | bytes 73760 | tf_op jit(solution)/shard_map/ppermute | solution.py:639
  21.2 4.4 %collective-permute-start.8 = (f32[9,8,256]{2,1,0:T(8,128)S(1)}, f32[9,8,256]{2,1,0:T(8,128)S(1)}, u32[]{:S(2)}, u32[]{:S(2)}) collective-permute-start(f32[9,8,256]{2,1,0:T(8,128)S(1)} %shard_map.130), channel_id=1, source_target_pairs={{0,12},{2,14},{4,8},{6,10},{8,4},{10,6},{12,0},{14,2},{1,13},{3,15... | collective-permute-start | bytes 221192 | tf_op jit(solution)/shard_map/ppermute | solution.py:639
  25.6 0.8 %collective-permute-start.6 = (f32[9,8,256]{2,1,0:T(8,128)S(1)}, f32[9,8,256]{2,1,0:T(8,128)S(1)}, u32[]{:S(2)}, u32[]{:S(2)}) collective-permute-start(f32[9,8,256]{2,1,0:T(8,128)S(1)} %shard_map.129), channel_id=1, source_target_pairs={{0,8},{2,10},{4,12},{6,14},{8,0},{10,2},{12,4},{14,6},{1,9},{3,11}... | collective-permute-start | bytes 221192 | tf_op jit(solution)/shard_map/ppermute | solution.py:639
  26.4 1.6 %collective-permute-start.4 = (f32[9,8,256]{2,1,0:T(8,128)S(1)}, f32[9,8,256]{2,1,0:T(8,128)S(1)}, u32[]{:S(2)}, u32[]{:S(2)}) collective-permute-start(f32[9,8,256]{2,1,0:T(8,128)S(1)} %shard_map.128), channel_id=1, source_target_pairs={{0,4},{2,6},{4,0},{6,2},{8,12},{10,14},{12,8},{14,10},{1,5},{3,7},... | collective-permute-start | bytes 221192 | tf_op jit(solution)/shard_map/ppermute | solution.py:639
  28.1 0.6 %collective-permute-done.8.refs_3_ = f32[9,8,256]{2,1,0:T(8,128)S(1)} collective-permute-done((f32[9,8,256]{2,1,0:T(8,128)S(1)}, f32[9,8,256]{2,1,0:T(8,128)S(1)}, u32[]{:S(2)}, u32[]{:S(2)}) %collective-permute-start.8) | collective-permute-done | bytes 73760 | tf_op jit(solution)/shard_map/ppermute | solution.py:639
  28.7 2.7 %collective-permute-done.6.refs_2_ = f32[9,8,256]{2,1,0:T(8,128)S(1)} collective-permute-done((f32[9,8,256]{2,1,0:T(8,128)S(1)}, f32[9,8,256]{2,1,0:T(8,128)S(1)}, u32[]{:S(2)}, u32[]{:S(2)}) %collective-permute-start.6) | collective-permute-done | bytes 73760 | tf_op jit(solution)/shard_map/ppermute | solution.py:639
  31.4 0.5 %collective-permute-done.4.refs_1_ = f32[9,8,256]{2,1,0:T(8,128)S(1)} collective-permute-done((f32[9,8,256]{2,1,0:T(8,128)S(1)}, f32[9,8,256]{2,1,0:T(8,128)S(1)}, u32[]{:S(2)}, u32[]{:S(2)}) %collective-permute-start.4) | collective-permute-done | bytes 73760 | tf_op jit(solution)/shard_map/ppermute | solution.py:639
  31.9 1.2 %collective-permute-start.13 = (f32[8,8,256]{2,1,0:T(8,128)S(1)}, f32[8,8,256]{2,1,0:T(8,128)S(1)}, u32[]{:S(2)}, u32[]{:S(2)}) collective-permute-start(f32[8,8,256]{2,1,0:T(8,128)S(1)} %shard_map.131.refs_0_), channel_id=1, source_target_pairs={{0,8},{2,10},{4,12},{6,14},{8,0},{10,2},{12,4},{14,6},{1,9},{3,11}... | collective-permute-start | bytes 196616 | tf_op jit(solution)/shard_map/ppermute | solution.py:639
  33.1 1.7 %collective-permute-start.11 = (f32[8,8,256]{2,1,0:T(8,128)S(1)}, f32[8,8,256]{2,1,0:T(8,128)S(1)}, u32[]{:S(2)}, u32[]{:S(2)}) collective-permute-start(f32[8,8,256]{2,1,0:T(8,128)S(1)} %shard_map.131.refs_0_), channel_id=1, source_target_pairs={{0,4},{2,6},{4,0},{6,2},{8,12},{10,14},{12,8},{14,10},{1,5},{3,7},... | collective-permute-start | bytes 196616 | tf_op jit(solution)/shard_map/ppermute | solution.py:639
  34.8 2.4 %collective-permute-start.10 = (f32[8,8,256]{2,1,0:T(8,128)S(1)}, f32[8,8,256]{2,1,0:T(8,128)S(1)}, u32[]{:S(2)}, u32[]{:S(2)}) collective-permute-start(f32[8,8,256]{2,1,0:T(8,128)S(1)} %shard_map.131.refs_0_), channel_id=1, source_target_pairs={{0,14},{2,12},{4,10},{6,8},{8,6},{10,4},{12,2},{14,0},{1,15},{3,13... | collective-permute-start | bytes 196616 | tf_op jit(solution)/shard_map/ppermute | solution.py:639
  37.2 0.6 %collective-permute-start.12 = (f32[8,8,256]{2,1,0:T(8,128)S(1)}, f32[8,8,256]{2,1,0:T(8,128)S(1)}, u32[]{:S(2)}, u32[]{:S(2)}) collective-permute-start(f32[8,8,256]{2,1,0:T(8,128)S(1)} %shard_map.131.refs_0_), channel_id=1, source_target_pairs={{0,2},{2,0},{4,6},{6,4},{8,10},{10,8},{12,14},{14,12},{1,3},{3,1},... | collective-permute-start | bytes 196616 | tf_op jit(solution)/shard_map/ppermute | solution.py:639
  37.8 2.2 %collective-permute-start.9 = (f32[8,8,256]{2,1,0:T(8,128)S(1)}, f32[8,8,256]{2,1,0:T(8,128)S(1)}, u32[]{:S(2)}, u32[]{:S(2)}) collective-permute-start(f32[8,8,256]{2,1,0:T(8,128)S(1)} %shard_map.131.refs_0_), channel_id=1, source_target_pairs={{0,12},{2,14},{4,8},{6,10},{8,4},{10,6},{12,0},{14,2},{1,13},{3,15... | collective-permute-start | bytes 196616 | tf_op jit(solution)/shard_map/ppermute | solution.py:639
  40.1 1.5 %collective-permute-start.14 = (f32[8,8,256]{2,1,0:T(8,128)S(1)}, f32[8,8,256]{2,1,0:T(8,128)S(1)}, u32[]{:S(2)}, u32[]{:S(2)}) collective-permute-start(f32[8,8,256]{2,1,0:T(8,128)S(1)} %collective-permute-done.13.refs_5_), channel_id=1, source_target_pairs={{0,2},{2,0},{4,6},{6,4},{8,10},{10,8},{12,14},{14,12},{1,3},{3,1},... | collective-permute-start | bytes 196616 | tf_op jit(solution)/shard_map/ppermute | solution.py:639
  41.6 0.6 %collective-permute-start.15 = (f32[8,8,256]{2,1,0:T(8,128)S(1)}, f32[8,8,256]{2,1,0:T(8,128)S(1)}, u32[]{:S(2)}, u32[]{:S(2)}) collective-permute-start(f32[8,8,256]{2,1,0:T(8,128)S(1)} %collective-permute-done.11.refs_3_), channel_id=1, source_target_pairs={{0,2},{2,0},{4,6},{6,4},{8,10},{10,8},{12,14},{14,12},{1,3},{3,1},... | collective-permute-start | bytes 196616 | tf_op jit(solution)/shard_map/ppermute | solution.py:639
  42.6 1.3 %collective-permute-done.9.refs_1_ = f32[8,8,256]{2,1,0:T(8,128)S(1)} collective-permute-done((f32[8,8,256]{2,1,0:T(8,128)S(1)}, f32[8,8,256]{2,1,0:T(8,128)S(1)}, u32[]{:S(2)}, u32[]{:S(2)}) %collective-permute-start.9) | collective-permute-done | bytes 65568 | tf_op jit(solution)/shard_map/ppermute | solution.py:639
  44.4 1.5 %collective-permute-done.15.refs_7_ = f32[8,8,256]{2,1,0:T(8,128)S(1)} collective-permute-done((f32[8,8,256]{2,1,0:T(8,128)S(1)}, f32[8,8,256]{2,1,0:T(8,128)S(1)}, u32[]{:S(2)}, u32[]{:S(2)}) %collective-permute-start.15) | collective-permute-done | bytes 65568 | tf_op jit(solution)/shard_map/ppermute | solution.py:639
  45.9 1.5 %shard_map.132 = (bf16[4,8,32,512]{3,2,1,0:T(8,128)(2,1)}, bf16[8,32,512]{2,1,0:T(8,128)(2,1)}) custom-call(s32[8,128]{1,0:T(8,128)S(1)} %broadcast_in_dim.4.counts_ref, f32[8,1,512]{2,1,0:T(1,128)S(1)} %broadcast_in_dim.10.relax_ref, bf16[4,7,32,512]{3,2,1,0:T(8,128)(2,1)S(1)} %get-tuple-element.17.adv_first_ref, ...), custom_call_target="tpu_custom_call" | custom-call | flops 2097152 | bytes 2097152 | tf_op jit(solution)/shard_map/pallas_call | solution.py:658
  (41 shorter events, 2.0 us)
Async XLA Ops:
  0.6 2.6 %copy-start.3 = (s32[1,32768]{1,0:T(1,128)S(1)}, s32[1,32768]{1,0:T(1,128)}, u32[]{:S(2)}) copy-start(s32[1,32768]{1,0:T(1,128)} %param.15) | copy-start | bytes 393220
  0.6 2.6 %copy-start.4 = (s32[1,32768]{1,0:T(1,128)S(1)}, s32[1,32768]{1,0:T(1,128)}, u32[]{:S(2)}) copy-start(s32[1,32768]{1,0:T(1,128)} %param.16) | copy-start | bytes 393220
  0.7 2.6 %copy-start.5 = (f32[1,32768]{1,0:T(1,128)S(1)}, f32[1,32768]{1,0:T(1,128)}, u32[]{:S(2)}) copy-start(f32[1,32768]{1,0:T(1,128)} %param.17) | copy-start | bytes 393220
  0.7 2.6 %copy-start.6 = (f32[1,32768]{1,0:T(1,128)S(1)}, f32[1,32768]{1,0:T(1,128)}, u32[]{:S(2)}) copy-start(f32[1,32768]{1,0:T(1,128)} %param.18) | copy-start | bytes 393220
  2.7 2.7 %collective-permute-start = (f32[34,8,512]{2,1,0:T(8,128)}, f32[34,8,512]{2,1,0:T(8,128)S(1)}, u32[]{:S(2)}, u32[]{:S(2)}) collective-permute-start(f32[34,8,512]{2,1,0:T(8,128)} %shard_map.122), channel_id=1, source_target_pairs={{0,1},{1,0},{2,3},{3,2},{4,5},{5,4},{6,7},{7,6},{8,9},{9,8},{10,11... | collective-permute-start | bytes 1671176 | tf_op jit(solution)/shard_map/ppermute | solution.py:547
  3.2 2.2 %copy-start = (bf16[4,8,32,512]{3,2,1,0:T(8,128)(2,1)S(1)}, bf16[4,8,32,512]{3,2,1,0:T(8,128)(2,1)}, u32[]{:S(2)}) copy-start(bf16[4,8,32,512]{3,2,1,0:T(8,128)(2,1)} %state_ref.3) | copy-start | bytes 3145732
  3.2 2.2 %copy-start.1 = (f32[32,512]{1,0:T(8,128)S(1)}, f32[32,512]{1,0:T(8,128)}, u32[]{:S(2)}) copy-start(f32[32,512]{1,0:T(8,128)} %east_ref.3) | copy-start | bytes 196612
  3.3 2.2 %copy-start.2 = (f32[32,512]{1,0:T(8,128)S(1)}, f32[32,512]{1,0:T(8,128)}, u32[]{:S(2)}) copy-start(f32[32,512]{1,0:T(8,128)} %north_ref.3) | copy-start | bytes 196612
  13.5 1.5 %collective-permute-start.1 = (f32[4,16,512]{2,1,0:T(8,128)S(1)}, f32[4,16,512]{2,1,0:T(8,128)S(1)}, u32[]{:S(2)}, u32[]{:S(2)}) collective-permute-start(f32[4,16,512]{2,1,0:T(8,128)S(1)} %get-tuple-element.19), channel_id=1, source_target_pairs={{0,1},{1,0},{2,3},{3,2},{4,5},{5,4},{6,7},{7,6},{8,9},{9,8},{10,11... | collective-permute-start | bytes 393224 | tf_op jit(solution)/shard_map/ppermute | solution.py:597
  15.0 30.8 %copy-start.9 = (f32[8]{0:T(128)S(1)}, f32[8]{0:T(128)}, u32[]{:S(2)}) copy-start(f32[8]{0:T(128)} %param.19) | copy-start | bytes 100
  15.5 5.7 %collective-permute-start.7 = (f32[9,8,256]{2,1,0:T(8,128)S(1)}, f32[9,8,256]{2,1,0:T(8,128)S(1)}, u32[]{:S(2)}, u32[]{:S(2)}) collective-permute-start(f32[9,8,256]{2,1,0:T(8,128)S(1)} %get-tuple-element.27), channel_id=1, source_target_pairs={{0,2},{2,0},{4,6},{6,4},{8,10},{10,8},{12,14},{14,12},{1,3},{3,1},... | collective-permute-start | bytes 221192 | tf_op jit(solution)/shard_map/ppermute | solution.py:639
  18.5 7.0 %collective-permute-start.5 = (f32[9,8,256]{2,1,0:T(8,128)S(1)}, f32[9,8,256]{2,1,0:T(8,128)S(1)}, u32[]{:S(2)}, u32[]{:S(2)}) collective-permute-start(f32[9,8,256]{2,1,0:T(8,128)S(1)} %get-tuple-element.25), channel_id=1, source_target_pairs={{0,2},{2,0},{4,6},{6,4},{8,10},{10,8},{12,14},{14,12},{1,3},{3,1},... | collective-permute-start | bytes 221192 | tf_op jit(solution)/shard_map/ppermute | solution.py:639
  18.6 7.8 %collective-permute-start.3 = (f32[9,8,256]{2,1,0:T(8,128)S(1)}, f32[9,8,256]{2,1,0:T(8,128)S(1)}, u32[]{:S(2)}, u32[]{:S(2)}) collective-permute-start(f32[9,8,256]{2,1,0:T(8,128)S(1)} %get-tuple-element.23), channel_id=1, source_target_pairs={{0,2},{2,0},{4,6},{6,4},{8,10},{10,8},{12,14},{14,12},{1,3},{3,1},... | collective-permute-start | bytes 221192 | tf_op jit(solution)/shard_map/ppermute | solution.py:639
  20.5 7.5 %collective-permute-start.2 = (f32[9,8,256]{2,1,0:T(8,128)S(1)}, f32[9,8,256]{2,1,0:T(8,128)S(1)}, u32[]{:S(2)}, u32[]{:S(2)}) collective-permute-start(f32[9,8,256]{2,1,0:T(8,128)S(1)} %get-tuple-element.21), channel_id=1, source_target_pairs={{0,2},{2,0},{4,6},{6,4},{8,10},{10,8},{12,14},{14,12},{1,3},{3,1},... | collective-permute-start | bytes 221192 | tf_op jit(solution)/shard_map/ppermute | solution.py:639
  21.2 7.5 %collective-permute-start.8 = (f32[9,8,256]{2,1,0:T(8,128)S(1)}, f32[9,8,256]{2,1,0:T(8,128)S(1)}, u32[]{:S(2)}, u32[]{:S(2)}) collective-permute-start(f32[9,8,256]{2,1,0:T(8,128)S(1)} %shard_map.130), channel_id=1, source_target_pairs={{0,12},{2,14},{4,8},{6,10},{8,4},{10,6},{12,0},{14,2},{1,13},{3,15... | collective-permute-start | bytes 221192 | tf_op jit(solution)/shard_map/ppermute | solution.py:639
  25.6 5.8 %collective-permute-start.6 = (f32[9,8,256]{2,1,0:T(8,128)S(1)}, f32[9,8,256]{2,1,0:T(8,128)S(1)}, u32[]{:S(2)}, u32[]{:S(2)}) collective-permute-start(f32[9,8,256]{2,1,0:T(8,128)S(1)} %shard_map.129), channel_id=1, source_target_pairs={{0,8},{2,10},{4,12},{6,14},{8,0},{10,2},{12,4},{14,6},{1,9},{3,11}... | collective-permute-start | bytes 221192 | tf_op jit(solution)/shard_map/ppermute | solution.py:639
  26.4 5.5 %collective-permute-start.4 = (f32[9,8,256]{2,1,0:T(8,128)S(1)}, f32[9,8,256]{2,1,0:T(8,128)S(1)}, u32[]{:S(2)}, u32[]{:S(2)}) collective-permute-start(f32[9,8,256]{2,1,0:T(8,128)S(1)} %shard_map.128), channel_id=1, source_target_pairs={{0,4},{2,6},{4,0},{6,2},{8,12},{10,14},{12,8},{14,10},{1,5},{3,7},... | collective-permute-start | bytes 221192 | tf_op jit(solution)/shard_map/ppermute | solution.py:639
  31.9 8.2 %collective-permute-start.13 = (f32[8,8,256]{2,1,0:T(8,128)S(1)}, f32[8,8,256]{2,1,0:T(8,128)S(1)}, u32[]{:S(2)}, u32[]{:S(2)}) collective-permute-start(f32[8,8,256]{2,1,0:T(8,128)S(1)} %shard_map.131.refs_0_), channel_id=1, source_target_pairs={{0,8},{2,10},{4,12},{6,14},{8,0},{10,2},{12,4},{14,6},{1,9},{3,11}... | collective-permute-start | bytes 196616 | tf_op jit(solution)/shard_map/ppermute | solution.py:639
  33.1 8.4 %collective-permute-start.11 = (f32[8,8,256]{2,1,0:T(8,128)S(1)}, f32[8,8,256]{2,1,0:T(8,128)S(1)}, u32[]{:S(2)}, u32[]{:S(2)}) collective-permute-start(f32[8,8,256]{2,1,0:T(8,128)S(1)} %shard_map.131.refs_0_), channel_id=1, source_target_pairs={{0,4},{2,6},{4,0},{6,2},{8,12},{10,14},{12,8},{14,10},{1,5},{3,7},... | collective-permute-start | bytes 196616 | tf_op jit(solution)/shard_map/ppermute | solution.py:639
  34.8 7.6 %collective-permute-start.10 = (f32[8,8,256]{2,1,0:T(8,128)S(1)}, f32[8,8,256]{2,1,0:T(8,128)S(1)}, u32[]{:S(2)}, u32[]{:S(2)}) collective-permute-start(f32[8,8,256]{2,1,0:T(8,128)S(1)} %shard_map.131.refs_0_), channel_id=1, source_target_pairs={{0,14},{2,12},{4,10},{6,8},{8,6},{10,4},{12,2},{14,0},{1,15},{3,13... | collective-permute-start | bytes 196616 | tf_op jit(solution)/shard_map/ppermute | solution.py:639
  37.2 5.4 %collective-permute-start.12 = (f32[8,8,256]{2,1,0:T(8,128)S(1)}, f32[8,8,256]{2,1,0:T(8,128)S(1)}, u32[]{:S(2)}, u32[]{:S(2)}) collective-permute-start(f32[8,8,256]{2,1,0:T(8,128)S(1)} %shard_map.131.refs_0_), channel_id=1, source_target_pairs={{0,2},{2,0},{4,6},{6,4},{8,10},{10,8},{12,14},{14,12},{1,3},{3,1},... | collective-permute-start | bytes 196616 | tf_op jit(solution)/shard_map/ppermute | solution.py:639
  37.8 6.1 %collective-permute-start.9 = (f32[8,8,256]{2,1,0:T(8,128)S(1)}, f32[8,8,256]{2,1,0:T(8,128)S(1)}, u32[]{:S(2)}, u32[]{:S(2)}) collective-permute-start(f32[8,8,256]{2,1,0:T(8,128)S(1)} %shard_map.131.refs_0_), channel_id=1, source_target_pairs={{0,12},{2,14},{4,8},{6,10},{8,4},{10,6},{12,0},{14,2},{1,13},{3,15... | collective-permute-start | bytes 196616 | tf_op jit(solution)/shard_map/ppermute | solution.py:639
  40.1 4.3 %collective-permute-start.14 = (f32[8,8,256]{2,1,0:T(8,128)S(1)}, f32[8,8,256]{2,1,0:T(8,128)S(1)}, u32[]{:S(2)}, u32[]{:S(2)}) collective-permute-start(f32[8,8,256]{2,1,0:T(8,128)S(1)} %collective-permute-done.13.refs_5_), channel_id=1, source_target_pairs={{0,2},{2,0},{4,6},{6,4},{8,10},{10,8},{12,14},{14,12},{1,3},{3,1},... | collective-permute-start | bytes 196616 | tf_op jit(solution)/shard_map/ppermute | solution.py:639
  41.6 4.3 %collective-permute-start.15 = (f32[8,8,256]{2,1,0:T(8,128)S(1)}, f32[8,8,256]{2,1,0:T(8,128)S(1)}, u32[]{:S(2)}, u32[]{:S(2)}) collective-permute-start(f32[8,8,256]{2,1,0:T(8,128)S(1)} %collective-permute-done.11.refs_3_), channel_id=1, source_target_pairs={{0,2},{2,0},{4,6},{6,4},{8,10},{10,8},{12,14},{14,12},{1,3},{3,1},... | collective-permute-start | bytes 196616 | tf_op jit(solution)/shard_map/ppermute | solution.py:639
  (2 other events, 4.3 us)
where the time goes:
time: 47.5 us; the launch traced here: 47.4 us
  starting transfers between devices  22.7 us (48%)
  Pallas kernels  14.9 us (31%)
  waiting for transfers between devices  8.08 us (17%)
  between operations  1.52 us (3%)
    ppermute x14, starting transfers between devices, swapped(): return lax.ppermute(x, 'mem', [(m, m ^ offset) for m in range(members)])  22.1 us
    pallas_call x1, Pallas kernels, on_device(): call(functools.partial(first_kernel, begin_steps), [VMEM] * 8, [((slots,...  8.08 us
    ppermute x14, waiting for transfers between devices, swapped(): return lax.ppermute(x, 'mem', [(m, m ^ offset) for m in range(members)])  8.07 us
    pallas_call x1, Pallas kernels, on_device(): call(functools.partial(begin_kernel, rows, width, begin_steps), [VMEM] *...  2.07 us
    pallas_call x1, Pallas kernels, on_device(): pl.pallas_call(edge_kernel, out_shape=[jax.ShapeDtypeStruct((slots * fiel...  2.02 us
    pallas_call x1, Pallas kernels, on_device(): pl.pallas_call(relax_kernel, out_shape=[jax.ShapeDtypeStruct(*out) for ou...  1.46 us
  transfers between devices with their start and end apart: 16, of which 9 were waited for; matrix products, arithmetic and copies ran while one was open for 0% of the time, Pallas kernels for 6%

commit v1 on v0

--- a/solution.py
+++ b/solution.py
@@ -367,7 +367,8 @@
         gains = [jnp.exp(score - peak) for score in scores]
         total = functools.reduce(jnp.add, gains)
         store(t, 0, peak + jnp.log(total))
-        gains = [gain / total for gain in gains]
+        scale = 1.0 / total
+        gains = [gain * scale for gain in gains]
         for f in range(fields):
             mean = None
             for s in range(slots):
@@ -410,7 +411,8 @@
         gains = [jnp.exp(score - peak) for score in scores]
         total = functools.reduce(jnp.add, gains)
         store(0, peak + jnp.log(total))
-        gains = [gain / total for gain in gains]
+        scale = 1.0 / total
+        gains = [gain * scale for gain in gains]
         for f in range(fields):
             mean = None
             for s in range(slots):
@@ -425,7 +427,8 @@
     peak = functools.reduce(jnp.maximum, [ref[0] for ref in refs])
     weights = [jnp.exp(ref[0] - peak) for ref in refs]
     total = functools.reduce(jnp.add, weights)
-    shares = [weight / total for weight in weights]
+    scale = 1.0 / total
+    shares = [weight * scale for weight in weights]
     means = [
         functools.reduce(jnp.add, [share * ref[q] for share, ref in zip(shares, refs)])
         for q in range(1, refs[0].shape[0])

time: 47.5 us -> 47.5 us (level)
  no operation moved by 1% of the time
where the time goes in v1:
time: 47.5 us; the launch traced here: 47.4 us
  starting transfers between devices  22.7 us (48%)
  Pallas kernels  14.9 us (31%)
  waiting for transfers between devices  8.08 us (17%)
  between operations  1.52 us (3%)
    ppermute x14, starting transfers between devices, swapped(): return lax.ppermute(x, 'mem', [(m, m ^ offset) for m in range(members)])  22.1 us
    pallas_call x1, Pallas kernels, on_device(): call(functools.partial(first_kernel, begin_steps), [VMEM] * 8, [((slots,...  8.08 us
    ppermute x14, waiting for transfers between devices, swapped(): return lax.ppermute(x, 'mem', [(m, m ^ offset) for m in range(members)])  8.07 us
    pallas_call x1, Pallas kernels, on_device(): call(functools.partial(begin_kernel, rows, width, begin_steps), [VMEM] *...  2.07 us
    pallas_call x1, Pallas kernels, on_device(): pl.pallas_call(edge_kernel, out_shape=[jax.ShapeDtypeStruct((slots * fiel...  2.02 us
    pallas_call x1, Pallas kernels, on_device(): pl.pallas_call(relax_kernel, out_shape=[jax.ShapeDtypeStruct(*out) for ou...  1.46 us
  transfers between devices with their start and end apart: 16, of which 9 were waited for; matrix products, arithmetic and copies ran while one was open for 0% of the time, Pallas kernels for 6%

profile of v1, /device:TPU:0, one launch (start us, length us, event | category | flops | bytes accessed | tf_op | source)
XLA Modules:
  0.0 47.4 jit_solution(12774251774280809742)
XLA Ops:
  0.7 2.0 %shard_map.122 = f32[34,8,512]{2,1,0:T(8,128)} custom-call(bf16[4,8,32,512]{3,2,1,0:T(8,128)(2,1)} %state_ref.3, f32[32,512]{1,0:T(8,128)} %east_ref.3, f32[32,512]{1,0:T(8,128)} %north_ref.3), custom_call_target="tpu_custom_call" | custom-call | bytes 786432 | tf_op jit(solution)/shard_map/pallas_call | solution.py:535
  2.7 0.5 %collective-permute-start = (f32[34,8,512]{2,1,0:T(8,128)}, f32[34,8,512]{2,1,0:T(8,128)S(1)}, u32[]{:S(2)}, u32[]{:S(2)}) collective-permute-start(f32[34,8,512]{2,1,0:T(8,128)} %shard_map.122), channel_id=1, source_target_pairs={{0,1},{1,0},{2,3},{3,2},{4,5},{5,4},{6,7},{7,6},{8,9},{9,8},{10,11... | collective-permute-start | bytes 1671176 | tf_op jit(solution)/shard_map/ppermute | solution.py:550
  3.3 2.1 %shard_map.123 = (f32[7,256,128]{2,1,0:T(8,128)S(1)}, f32[320,256]{1,0:T(8,128)S(1)}) custom-call(s32[256,128]{1,0:T(8,128)S(1)} %bitcast.5, s32[256,128]{1,0:T(8,128)S(1)} %bitcast.6, f32[256,128]{1,0:T(8,128)S(1)} %bitcast.7, f32[256,128]{1,0:T(8,128)S(1)} %bitcast.8), custom_call_target="tpu_custom_call" | custom-call | flops 1342177280 | bytes 524288 | tf_op jit(solution)/shard_map/pallas_call | solution.py:560
  5.4 8.1 %shard_map.124 = (bf16[4,7,32,512]{3,2,1,0:T(8,128)(2,1)S(1)}, f32[4,32,512]{2,1,0:T(8,128)S(1)}, f32[4,16,512]{2,1,0:T(8,128)S(1)}) custom-call(bf16[4,8,32,512]{3,2,1,0:T(8,128)(2,1)S(1)} %copy-done, f32[34,8,512]{2,1,0:T(8,128)S(1)} %collective-permute-done.halo_ref, f32[32,512]{1,0:T(8,128)S(1)} %copy-done.1, f32[32,512]{1,0:T(8,128)S(1)} %copy-done.2, ...), custom_call_target="tpu_custom_call" | custom-call | flops 4055891968 | bytes 1048576 | tf_op jit(solution)/shard_map/pallas_call | solution.py:587
  14.3 0.7 %shard_map.125.adv_rest_ref = bf16[4,1,32,512]{3,2,1,0:T(8,128)(2,1)S(1)} custom-call(bf16[4,8,32,512]{3,2,1,0:T(8,128)(2,1)S(1)} %copy-done, f32[34,8,512]{2,1,0:T(8,128)S(1)} %collective-permute-done.halo_ref, f32[32,512]{1,0:T(8,128)S(1)} %copy-done.1, f32[32,512]{1,0:T(8,128)S(1)} %copy-done.2), custom_call_target="tpu_custom_call" | custom-call | flops 4194304 | bytes 2097152 | tf_op jit(solution)/shard_map/pallas_call | solution.py:602
  15.5 3.0 %collective-permute-start.7 = (f32[9,8,256]{2,1,0:T(8,128)S(1)}, f32[9,8,256]{2,1,0:T(8,128)S(1)}, u32[]{:S(2)}, u32[]{:S(2)}) collective-permute-start(f32[9,8,256]{2,1,0:T(8,128)S(1)} %get-tuple-element.27), channel_id=1, source_target_pairs={{0,2},{2,0},{4,6},{6,4},{8,10},{10,8},{12,14},{14,12},{1,3},{3,1},... | collective-permute-start | bytes 221192 | tf_op jit(solution)/shard_map/ppermute | solution.py:642
  18.6 1.9 %collective-permute-start.3 = (f32[9,8,256]{2,1,0:T(8,128)S(1)}, f32[9,8,256]{2,1,0:T(8,128)S(1)}, u32[]{:S(2)}, u32[]{:S(2)}) collective-permute-start(f32[9,8,256]{2,1,0:T(8,128)S(1)} %get-tuple-element.23), channel_id=1, source_target_pairs={{0,2},{2,0},{4,6},{6,4},{8,10},{10,8},{12,14},{14,12},{1,3},{3,1},... | collective-permute-start | bytes 221192 | tf_op jit(solution)/shard_map/ppermute | solution.py:642
  20.6 0.5 %collective-permute-done.7.refs_1_ = f32[9,8,256]{2,1,0:T(8,128)S(1)} collective-permute-done((f32[9,8,256]{2,1,0:T(8,128)S(1)}, f32[9,8,256]{2,1,0:T(8,128)S(1)}, u32[]{:S(2)}, u32[]{:S(2)}) %collective-permute-start.7) | collective-permute-done | bytes 73760 | tf_op jit(solution)/shard_map/ppermute | solution.py:642
  21.2 4.4 %collective-permute-start.8 = (f32[9,8,256]{2,1,0:T(8,128)S(1)}, f32[9,8,256]{2,1,0:T(8,128)S(1)}, u32[]{:S(2)}, u32[]{:S(2)}) collective-permute-start(f32[9,8,256]{2,1,0:T(8,128)S(1)} %shard_map.130), channel_id=1, source_target_pairs={{0,12},{2,14},{4,8},{6,10},{8,4},{10,6},{12,0},{14,2},{1,13},{3,15... | collective-permute-start | bytes 221192 | tf_op jit(solution)/shard_map/ppermute | solution.py:642
  25.6 0.8 %collective-permute-start.6 = (f32[9,8,256]{2,1,0:T(8,128)S(1)}, f32[9,8,256]{2,1,0:T(8,128)S(1)}, u32[]{:S(2)}, u32[]{:S(2)}) collective-permute-start(f32[9,8,256]{2,1,0:T(8,128)S(1)} %shard_map.129), channel_id=1, source_target_pairs={{0,8},{2,10},{4,12},{6,14},{8,0},{10,2},{12,4},{14,6},{1,9},{3,11}... | collective-permute-start | bytes 221192 | tf_op jit(solution)/shard_map/ppermute | solution.py:642
  26.4 1.6 %collective-permute-start.4 = (f32[9,8,256]{2,1,0:T(8,128)S(1)}, f32[9,8,256]{2,1,0:T(8,128)S(1)}, u32[]{:S(2)}, u32[]{:S(2)}) collective-permute-start(f32[9,8,256]{2,1,0:T(8,128)S(1)} %shard_map.128), channel_id=1, source_target_pairs={{0,4},{2,6},{4,0},{6,2},{8,12},{10,14},{12,8},{14,10},{1,5},{3,7},... | collective-permute-start | bytes 221192 | tf_op jit(solution)/shard_map/ppermute | solution.py:642
  28.1 0.6 %collective-permute-done.8.refs_3_ = f32[9,8,256]{2,1,0:T(8,128)S(1)} collective-permute-done((f32[9,8,256]{2,1,0:T(8,128)S(1)}, f32[9,8,256]{2,1,0:T(8,128)S(1)}, u32[]{:S(2)}, u32[]{:S(2)}) %collective-permute-start.8) | collective-permute-done | bytes 73760 | tf_op jit(solution)/shard_map/ppermute | solution.py:642
  28.7 2.7 %collective-permute-done.6.refs_2_ = f32[9,8,256]{2,1,0:T(8,128)S(1)} collective-permute-done((f32[9,8,256]{2,1,0:T(8,128)S(1)}, f32[9,8,256]{2,1,0:T(8,128)S(1)}, u32[]{:S(2)}, u32[]{:S(2)}) %collective-permute-start.6) | collective-permute-done | bytes 73760 | tf_op jit(solution)/shard_map/ppermute | solution.py:642
  31.4 0.5 %collective-permute-done.4.refs_1_ = f32[9,8,256]{2,1,0:T(8,128)S(1)} collective-permute-done((f32[9,8,256]{2,1,0:T(8,128)S(1)}, f32[9,8,256]{2,1,0:T(8,128)S(1)}, u32[]{:S(2)}, u32[]{:S(2)}) %collective-permute-start.4) | collective-permute-done | bytes 73760 | tf_op jit(solution)/shard_map/ppermute | solution.py:642
  31.9 1.2 %collective-permute-start.13 = (f32[8,8,256]{2,1,0:T(8,128)S(1)}, f32[8,8,256]{2,1,0:T(8,128)S(1)}, u32[]{:S(2)}, u32[]{:S(2)}) collective-permute-start(f32[8,8,256]{2,1,0:T(8,128)S(1)} %shard_map.131.refs_0_), channel_id=1, source_target_pairs={{0,8},{2,10},{4,12},{6,14},{8,0},{10,2},{12,4},{14,6},{1,9},{3,11}... | collective-permute-start | bytes 196616 | tf_op jit(solution)/shard_map/ppermute | solution.py:642
  33.1 1.7 %collective-permute-start.11 = (f32[8,8,256]{2,1,0:T(8,128)S(1)}, f32[8,8,256]{2,1,0:T(8,128)S(1)}, u32[]{:S(2)}, u32[]{:S(2)}) collective-permute-start(f32[8,8,256]{2,1,0:T(8,128)S(1)} %shard_map.131.refs_0_), channel_id=1, source_target_pairs={{0,4},{2,6},{4,0},{6,2},{8,12},{10,14},{12,8},{14,10},{1,5},{3,7},... | collective-permute-start | bytes 196616 | tf_op jit(solution)/shard_map/ppermute | solution.py:642
  34.8 2.4 %collective-permute-start.10 = (f32[8,8,256]{2,1,0:T(8,128)S(1)}, f32[8,8,256]{2,1,0:T(8,128)S(1)}, u32[]{:S(2)}, u32[]{:S(2)}) collective-permute-start(f32[8,8,256]{2,1,0:T(8,128)S(1)} %shard_map.131.refs_0_), channel_id=1, source_target_pairs={{0,14},{2,12},{4,10},{6,8},{8,6},{10,4},{12,2},{14,0},{1,15},{3,13... | collective-permute-start | bytes 196616 | tf_op jit(solution)/shard_map/ppermute | solution.py:642
  37.2 0.6 %collective-permute-start.12 = (f32[8,8,256]{2,1,0:T(8,128)S(1)}, f32[8,8,256]{2,1,0:T(8,128)S(1)}, u32[]{:S(2)}, u32[]{:S(2)}) collective-permute-start(f32[8,8,256]{2,1,0:T(8,128)S(1)} %shard_map.131.refs_0_), channel_id=1, source_target_pairs={{0,2},{2,0},{4,6},{6,4},{8,10},{10,8},{12,14},{14,12},{1,3},{3,1},... | collective-permute-start | bytes 196616 | tf_op jit(solution)/shard_map/ppermute | solution.py:642
  37.8 2.2 %collective-permute-start.9 = (f32[8,8,256]{2,1,0:T(8,128)S(1)}, f32[8,8,256]{2,1,0:T(8,128)S(1)}, u32[]{:S(2)}, u32[]{:S(2)}) collective-permute-start(f32[8,8,256]{2,1,0:T(8,128)S(1)} %shard_map.131.refs_0_), channel_id=1, source_target_pairs={{0,12},{2,14},{4,8},{6,10},{8,4},{10,6},{12,0},{14,2},{1,13},{3,15... | collective-permute-start | bytes 196616 | tf_op jit(solution)/shard_map/ppermute | solution.py:642
  40.1 1.5 %collective-permute-start.14 = (f32[8,8,256]{2,1,0:T(8,128)S(1)}, f32[8,8,256]{2,1,0:T(8,128)S(1)}, u32[]{:S(2)}, u32[]{:S(2)}) collective-permute-start(f32[8,8,256]{2,1,0:T(8,128)S(1)} %collective-permute-done.13.refs_5_), channel_id=1, source_target_pairs={{0,2},{2,0},{4,6},{6,4},{8,10},{10,8},{12,14},{14,12},{1,3},{3,1},... | collective-permute-start | bytes 196616 | tf_op jit(solution)/shard_map/ppermute | solution.py:642
  41.6 0.6 %collective-permute-start.15 = (f32[8,8,256]{2,1,0:T(8,128)S(1)}, f32[8,8,256]{2,1,0:T(8,128)S(1)}, u32[]{:S(2)}, u32[]{:S(2)}) collective-permute-start(f32[8,8,256]{2,1,0:T(8,128)S(1)} %collective-permute-done.11.refs_3_), channel_id=1, source_target_pairs={{0,2},{2,0},{4,6},{6,4},{8,10},{10,8},{12,14},{14,12},{1,3},{3,1},... | collective-permute-start | bytes 196616 | tf_op jit(solution)/shard_map/ppermute | solution.py:642
  42.6 1.3 %collective-permute-done.9.refs_1_ = f32[8,8,256]{2,1,0:T(8,128)S(1)} collective-permute-done((f32[8,8,256]{2,1,0:T(8,128)S(1)}, f32[8,8,256]{2,1,0:T(8,128)S(1)}, u32[]{:S(2)}, u32[]{:S(2)}) %collective-permute-start.9) | collective-permute-done | bytes 65568 | tf_op jit(solution)/shard_map/ppermute | solution.py:642
  44.4 1.5 %collective-permute-done.15.refs_7_ = f32[8,8,256]{2,1,0:T(8,128)S(1)} collective-permute-done((f32[8,8,256]{2,1,0:T(8,128)S(1)}, f32[8,8,256]{2,1,0:T(8,128)S(1)}, u32[]{:S(2)}, u32[]{:S(2)}) %collective-permute-start.15) | collective-permute-done | bytes 65568 | tf_op jit(solution)/shard_map/ppermute | solution.py:642
  45.9 1.5 %shard_map.132 = (bf16[4,8,32,512]{3,2,1,0:T(8,128)(2,1)}, bf16[8,32,512]{2,1,0:T(8,128)(2,1)}) custom-call(s32[8,128]{1,0:T(8,128)S(1)} %broadcast_in_dim.4.counts_ref, f32[8,1,512]{2,1,0:T(1,128)S(1)} %broadcast_in_dim.10.relax_ref, bf16[4,7,32,512]{3,2,1,0:T(8,128)(2,1)S(1)} %get-tuple-element.17.adv_first_ref, ...), custom_call_target="tpu_custom_call" | custom-call | flops 2097152 | bytes 2097152 | tf_op jit(solution)/shard_map/pallas_call | solution.py:661
  (41 shorter events, 2.0 us)
Async XLA Ops:
  0.6 2.6 %copy-start.3 = (s32[1,32768]{1,0:T(1,128)S(1)}, s32[1,32768]{1,0:T(1,128)}, u32[]{:S(2)}) copy-start(s32[1,32768]{1,0:T(1,128)} %param.15) | copy-start | bytes 393220
  0.6 2.6 %copy-start.4 = (s32[1,32768]{1,0:T(1,128)S(1)}, s32[1,32768]{1,0:T(1,128)}, u32[]{:S(2)}) copy-start(s32[1,32768]{1,0:T(1,128)} %param.16) | copy-start | bytes 393220
  0.7 2.6 %copy-start.5 = (f32[1,32768]{1,0:T(1,128)S(1)}, f32[1,32768]{1,0:T(1,128)}, u32[]{:S(2)}) copy-start(f32[1,32768]{1,0:T(1,128)} %param.17) | copy-start | bytes 393220
  0.7 2.6 %copy-start.6 = (f32[1,32768]{1,0:T(1,128)S(1)}, f32[1,32768]{1,0:T(1,128)}, u32[]{:S(2)}) copy-start(f32[1,32768]{1,0:T(1,128)} %param.18) | copy-start | bytes 393220
  2.7 2.7 %collective-permute-start = (f32[34,8,512]{2,1,0:T(8,128)}, f32[34,8,512]{2,1,0:T(8,128)S(1)}, u32[]{:S(2)}, u32[]{:S(2)}) collective-permute-start(f32[34,8,512]{2,1,0:T(8,128)} %shard_map.122), channel_id=1, source_target_pairs={{0,1},{1,0},{2,3},{3,2},{4,5},{5,4},{6,7},{7,6},{8,9},{9,8},{10,11... | collective-permute-start | bytes 1671176 | tf_op jit(solution)/shard_map/ppermute | solution.py:550
  3.2 2.2 %copy-start = (bf16[4,8,32,512]{3,2,1,0:T(8,128)(2,1)S(1)}, bf16[4,8,32,512]{3,2,1,0:T(8,128)(2,1)}, u32[]{:S(2)}) copy-start(bf16[4,8,32,512]{3,2,1,0:T(8,128)(2,1)} %state_ref.3) | copy-start | bytes 3145732
  3.2 2.2 %copy-start.1 = (f32[32,512]{1,0:T(8,128)S(1)}, f32[32,512]{1,0:T(8,128)}, u32[]{:S(2)}) copy-start(f32[32,512]{1,0:T(8,128)} %east_ref.3) | copy-start | bytes 196612
  3.3 2.2 %copy-start.2 = (f32[32,512]{1,0:T(8,128)S(1)}, f32[32,512]{1,0:T(8,128)}, u32[]{:S(2)}) copy-start(f32[32,512]{1,0:T(8,128)} %north_ref.3) | copy-start | bytes 196612
  13.5 1.5 %collective-permute-start.1 = (f32[4,16,512]{2,1,0:T(8,128)S(1)}, f32[4,16,512]{2,1,0:T(8,128)S(1)}, u32[]{:S(2)}, u32[]{:S(2)}) collective-permute-start(f32[4,16,512]{2,1,0:T(8,128)S(1)} %get-tuple-element.19), channel_id=1, source_target_pairs={{0,1},{1,0},{2,3},{3,2},{4,5},{5,4},{6,7},{7,6},{8,9},{9,8},{10,11... | collective-permute-start | bytes 393224 | tf_op jit(solution)/shard_map/ppermute | solution.py:600
  15.0 30.8 %copy-start.9 = (f32[8]{0:T(128)S(1)}, f32[8]{0:T(128)}, u32[]{:S(2)}) copy-start(f32[8]{0:T(128)} %param.19) | copy-start | bytes 100
  15.5 5.7 %collective-permute-start.7 = (f32[9,8,256]{2,1,0:T(8,128)S(1)}, f32[9,8,256]{2,1,0:T(8,128)S(1)}, u32[]{:S(2)}, u32[]{:S(2)}) collective-permute-start(f32[9,8,256]{2,1,0:T(8,128)S(1)} %get-tuple-element.27), channel_id=1, source_target_pairs={{0,2},{2,0},{4,6},{6,4},{8,10},{10,8},{12,14},{14,12},{1,3},{3,1},... | collective-permute-start | bytes 221192 | tf_op jit(solution)/shard_map/ppermute | solution.py:642
  18.5 7.0 %collective-permute-start.5 = (f32[9,8,256]{2,1,0:T(8,128)S(1)}, f32[9,8,256]{2,1,0:T(8,128)S(1)}, u32[]{:S(2)}, u32[]{:S(2)}) collective-permute-start(f32[9,8,256]{2,1,0:T(8,128)S(1)} %get-tuple-element.25), channel_id=1, source_target_pairs={{0,2},{2,0},{4,6},{6,4},{8,10},{10,8},{12,14},{14,12},{1,3},{3,1},... | collective-permute-start | bytes 221192 | tf_op jit(solution)/shard_map/ppermute | solution.py:642
  18.6 7.8 %collective-permute-start.3 = (f32[9,8,256]{2,1,0:T(8,128)S(1)}, f32[9,8,256]{2,1,0:T(8,128)S(1)}, u32[]{:S(2)}, u32[]{:S(2)}) collective-permute-start(f32[9,8,256]{2,1,0:T(8,128)S(1)} %get-tuple-element.23), channel_id=1, source_target_pairs={{0,2},{2,0},{4,6},{6,4},{8,10},{10,8},{12,14},{14,12},{1,3},{3,1},... | collective-permute-start | bytes 221192 | tf_op jit(solution)/shard_map/ppermute | solution.py:642
  20.5 7.5 %collective-permute-start.2 = (f32[9,8,256]{2,1,0:T(8,128)S(1)}, f32[9,8,256]{2,1,0:T(8,128)S(1)}, u32[]{:S(2)}, u32[]{:S(2)}) collective-permute-start(f32[9,8,256]{2,1,0:T(8,128)S(1)} %get-tuple-element.21), channel_id=1, source_target_pairs={{0,2},{2,0},{4,6},{6,4},{8,10},{10,8},{12,14},{14,12},{1,3},{3,1},... | collective-permute-start | bytes 221192 | tf_op jit(solution)/shard_map/ppermute | solution.py:642
  21.2 7.5 %collective-permute-start.8 = (f32[9,8,256]{2,1,0:T(8,128)S(1)}, f32[9,8,256]{2,1,0:T(8,128)S(1)}, u32[]{:S(2)}, u32[]{:S(2)}) collective-permute-start(f32[9,8,256]{2,1,0:T(8,128)S(1)} %shard_map.130), channel_id=1, source_target_pairs={{0,12},{2,14},{4,8},{6,10},{8,4},{10,6},{12,0},{14,2},{1,13},{3,15... | collective-permute-start | bytes 221192 | tf_op jit(solution)/shard_map/ppermute | solution.py:642
  25.6 5.8 %collective-permute-start.6 = (f32[9,8,256]{2,1,0:T(8,128)S(1)}, f32[9,8,256]{2,1,0:T(8,128)S(1)}, u32[]{:S(2)}, u32[]{:S(2)}) collective-permute-start(f32[9,8,256]{2,1,0:T(8,128)S(1)} %shard_map.129), channel_id=1, source_target_pairs={{0,8},{2,10},{4,12},{6,14},{8,0},{10,2},{12,4},{14,6},{1,9},{3,11}... | collective-permute-start | bytes 221192 | tf_op jit(solution)/shard_map/ppermute | solution.py:642
  26.4 5.5 %collective-permute-start.4 = (f32[9,8,256]{2,1,0:T(8,128)S(1)}, f32[9,8,256]{2,1,0:T(8,128)S(1)}, u32[]{:S(2)}, u32[]{:S(2)}) collective-permute-start(f32[9,8,256]{2,1,0:T(8,128)S(1)} %shard_map.128), channel_id=1, source_target_pairs={{0,4},{2,6},{4,0},{6,2},{8,12},{10,14},{12,8},{14,10},{1,5},{3,7},... | collective-permute-start | bytes 221192 | tf_op jit(solution)/shard_map/ppermute | solution.py:642
  31.9 8.2 %collective-permute-start.13 = (f32[8,8,256]{2,1,0:T(8,128)S(1)}, f32[8,8,256]{2,1,0:T(8,128)S(1)}, u32[]{:S(2)}, u32[]{:S(2)}) collective-permute-start(f32[8,8,256]{2,1,0:T(8,128)S(1)} %shard_map.131.refs_0_), channel_id=1, source_target_pairs={{0,8},{2,10},{4,12},{6,14},{8,0},{10,2},{12,4},{14,6},{1,9},{3,11}... | collective-permute-start | bytes 196616 | tf_op jit(solution)/shard_map/ppermute | solution.py:642
  33.1 8.4 %collective-permute-start.11 = (f32[8,8,256]{2,1,0:T(8,128)S(1)}, f32[8,8,256]{2,1,0:T(8,128)S(1)}, u32[]{:S(2)}, u32[]{:S(2)}) collective-permute-start(f32[8,8,256]{2,1,0:T(8,128)S(1)} %shard_map.131.refs_0_), channel_id=1, source_target_pairs={{0,4},{2,6},{4,0},{6,2},{8,12},{10,14},{12,8},{14,10},{1,5},{3,7},... | collective-permute-start | bytes 196616 | tf_op jit(solution)/shard_map/ppermute | solution.py:642
  34.8 7.6 %collective-permute-start.10 = (f32[8,8,256]{2,1,0:T(8,128)S(1)}, f32[8,8,256]{2,1,0:T(8,128)S(1)}, u32[]{:S(2)}, u32[]{:S(2)}) collective-permute-start(f32[8,8,256]{2,1,0:T(8,128)S(1)} %shard_map.131.refs_0_), channel_id=1, source_target_pairs={{0,14},{2,12},{4,10},{6,8},{8,6},{10,4},{12,2},{14,0},{1,15},{3,13... | collective-permute-start | bytes 196616 | tf_op jit(solution)/shard_map/ppermute | solution.py:642
  37.2 5.4 %collective-permute-start.12 = (f32[8,8,256]{2,1,0:T(8,128)S(1)}, f32[8,8,256]{2,1,0:T(8,128)S(1)}, u32[]{:S(2)}, u32[]{:S(2)}) collective-permute-start(f32[8,8,256]{2,1,0:T(8,128)S(1)} %shard_map.131.refs_0_), channel_id=1, source_target_pairs={{0,2},{2,0},{4,6},{6,4},{8,10},{10,8},{12,14},{14,12},{1,3},{3,1},... | collective-permute-start | bytes 196616 | tf_op jit(solution)/shard_map/ppermute | solution.py:642
  37.8 6.1 %collective-permute-start.9 = (f32[8,8,256]{2,1,0:T(8,128)S(1)}, f32[8,8,256]{2,1,0:T(8,128)S(1)}, u32[]{:S(2)}, u32[]{:S(2)}) collective-permute-start(f32[8,8,256]{2,1,0:T(8,128)S(1)} %shard_map.131.refs_0_), channel_id=1, source_target_pairs={{0,12},{2,14},{4,8},{6,10},{8,4},{10,6},{12,0},{14,2},{1,13},{3,15... | collective-permute-start | bytes 196616 | tf_op jit(solution)/shard_map/ppermute | solution.py:642
  40.1 4.3 %collective-permute-start.14 = (f32[8,8,256]{2,1,0:T(8,128)S(1)}, f32[8,8,256]{2,1,0:T(8,128)S(1)}, u32[]{:S(2)}, u32[]{:S(2)}) collective-permute-start(f32[8,8,256]{2,1,0:T(8,128)S(1)} %collective-permute-done.13.refs_5_), channel_id=1, source_target_pairs={{0,2},{2,0},{4,6},{6,4},{8,10},{10,8},{12,14},{14,12},{1,3},{3,1},... | collective-permute-start | bytes 196616 | tf_op jit(solution)/shard_map/ppermute | solution.py:642
  41.6 4.3 %collective-permute-start.15 = (f32[8,8,256]{2,1,0:T(8,128)S(1)}, f32[8,8,256]{2,1,0:T(8,128)S(1)}, u32[]{:S(2)}, u32[]{:S(2)}) collective-permute-start(f32[8,8,256]{2,1,0:T(8,128)S(1)} %collective-permute-done.11.refs_3_), channel_id=1, source_target_pairs={{0,2},{2,0},{4,6},{6,4},{8,10},{10,8},{12,14},{14,12},{1,3},{3,1},... | collective-permute-start | bytes 196616 | tf_op jit(solution)/shard_map/ppermute | solution.py:642
  (2 other events, 4.3 us)
